TPU v7x, 32 devices: a whole 2x2x4 slice. The times are simulated.
32 devices in a mesh: shard: 4 (over y, x), node: 4 (over z), replica: 2 (over core).
Axes of the slice: x: 2, y: 2, z: 4, core: 2. Of those that a mesh axis runs over, the one named last changes fastest.
Arguments:
- tokens: bfloat16 [6144, 8192], P(('shard', 'node', 'replica')), may hold values from -6 to 6
- weight_codes: bfloat16 [8192, 256], P('shard'), may hold values from -4 to 4
- scale_powers: int32 [64, 256], replicated, may hold values from 5 to 8
- cotangent: bfloat16 [6144, 256], P(('shard', 'node', 'replica')), may hold values from -0.078125 to 0.078125
Outputs:
- keys_values: bfloat16 [6144, 256], P(('shard', 'node', 'replica'))
- weight_grad: float32 [8192, 256], P(('shard', 'node', 'replica'))
All inputs are finite; a program needn't handle non-finite values.
Results may differ from a plain program's by a relative error of at most 0.0028.
Values may be sent and summed in bfloat16 or wider, within the bound.
A program may use at most 64 MiB of HBM per device.

v0:
```python
import jax
import jax.numpy as jnp
from jax import lax
from jax.sharding import PartitionSpec as P

BLOCK = 128


def on_device(tokens, weight_codes, scale_powers, cotangent):
    factors = jnp.repeat(jnp.exp2(-scale_powers.astype(jnp.float32)), BLOCK, axis=0)
    codes = lax.all_gather(weight_codes, "shard", axis=0, tiled=True)
    weight = (codes.astype(jnp.float32) * factors).astype(jnp.bfloat16)
    projected = jnp.dot(tokens, weight, preferred_element_type=jnp.float32)
    keys_values = projected.astype(jnp.bfloat16)
    partial_value = lax.dot_general(
        tokens, cotangent, (((0,), (0,)), ((), ())), preferred_element_type=jnp.float32
    )
    inner = lax.psum_scatter(partial_value, "shard", scatter_dimension=0, tiled=True)
    weight_grad = lax.psum_scatter(inner, ("node", "replica"), scatter_dimension=0, tiled=True)
    return (keys_values, weight_grad)


def solution(mesh):
    placed = (
        P(("shard", "node", "replica"), None),
        P("shard", None),
        P(),
        P(("shard", "node", "replica"), None),
    )
    return jax.shard_map(
        on_device,
        mesh=mesh,
        in_specs=placed,
        out_specs=(P(("shard", "node", "replica"), None), P(("shard", "node", "replica"), None)),
        check_vma=False,
    )
```

profile of v0, /device:TPU:0, one launch (start us, length us, event | category | flops | bytes accessed | tf_op | source)
XLA Modules:
  0.0 203.9 jit_solution(7095306951744041823)
XLA Ops:
  7.2 0.0 copy-start
  7.2 0.0 reduce-scatter.3.cloned.1.call-start
  7.2 1.8 copy-done
  9.1 5.5 %fusion.2 = f32[8192,256]{1,0:T(8,128)} fusion(bf16[192,8192]{1,0:T(8,128)(2,1)S(1)} %copy-done, bf16[192,256]{1,0:T(8,128)(2,1)} %param.7), kind=kOutput, calls=%fused_computation.5 | convolution fusion | flops 805306368 | bytes 11632640 | tf_op jit(solution)/shard_map/dot_general | solution.py:15
  14.5 0.0 copy-start.1
  14.5 0.0 reduce-scatter.3.cloned.1.call-update
  14.5 0.0 all-gather.2.cloned.1.call-start
  14.6 0.7 all-gather.2.cloned.1.call-update
  15.3 0.0 reduce-scatter.5.cloned.1.call-start
  15.3 88.5 %reduce-scatter.3.cloned.1.call-done = f32[2048,256]{1,0:T(8,128)} async-done(((f32[8192,256]{1,0:T(8,128)}), f32[2048,256]{1,0:T(8,128)}) %reduce-scatter.3.cloned.1.call-update) | async-done | bytes 2097168 | tf_op jit(solution)/shard_map/reduce_scatter | solution.py:18
  103.8 0.0 reduce-scatter.5.cloned.1.call-update
  103.8 0.0 copy-done.1
  103.9 54.6 %all-gather.2.cloned.1.call-done = bf16[8192,256]{1,0:T(8,128)(2,1)} async-done(((bf16[2048,256]{1,0:T(8,128)(2,1)}), bf16[8192,256]{1,0:T(8,128)(2,1)}) %all-gather.2.cloned.1.call-update) | async-done | bytes 4194320 | tf_op jit(solution)/shard_map/all_gather | solution.py:11
  158.5 3.0 %fusion = bf16[8192,256]{1,0:T(8,128)(2,1)S(1)} fusion(bf16[8192,256]{1,0:T(8,128)(2,1)} %all-gather.2.cloned.1.call-done, f32[64,256]{1,0:T(8,128)S(1)} %multiply_exponential_fusion), kind=kLoop, calls=%fused_computation.1 | loop fusion | flops 6291456 | bytes 8454144 | tf_op jit(solution)/shard_map/convert_element_type | solution.py:12
  161.5 1.7 fusion.1
  163.2 34.2 %reduce-scatter.5.cloned.1.call-done = f32[256,256]{1,0:T(8,128)} async-done(((f32[2048,256]{1,0:T(8,128)}), f32[256,256]{1,0:T(8,128)}) %reduce-scatter.5.cloned.1.call-update) | async-done | bytes 262160 | tf_op jit(solution)/shard_map/reduce_scatter | solution.py:19
  (1 shorter events, 0.0 us)
Async XLA Ops:
  7.2 1.9 copy-start
  7.2 96.6 %reduce-scatter.3.cloned.1.call-start = ((), (), s32[]{:S(2)}) async-start(), calls=%async_computation.3 | async-start | bytes 10485760 | tf_op jit(solution)/shard_map/reduce_scatter | solution.py:18
  14.5 89.3 %copy-start.1 = (s32[64,256]{1,0:T(8,128)S(1)}, s32[64,256]{1,0:T(8,128)}, u32[]{:S(2)}) copy-start(s32[64,256]{1,0:T(8,128)} %param.6) | copy-start | bytes 196612
  14.5 144.0 %all-gather.2.cloned.1.call-start = ((), (), s32[]{:S(2)}) async-start(), calls=%async_computation.2 | async-start | bytes 5242880 | tf_op jit(solution)/shard_map/all_gather | solution.py:11
  15.3 182.1 %reduce-scatter.5.cloned.1.call-start = ((), (), s32[]{:S(2)}) async-start(), calls=%async_computation.4 | async-start | bytes 2359296 | tf_op jit(solution)/shard_map/reduce_scatter | solution.py:19
Sparse Core Ops, SparseCore 0:
  14.7 89.0 reduce-scatter.2
  105.8 52.6 all-gather.1
  161.5 35.8 reduce-scatter.4
where the time goes:
time: 204 us
  waiting for transfers between devices  178 us (87%)
  between operations  13.8 us (7%)
  matrix products  7.16 us (4%)
  other arithmetic  3.04 us (1%)
    reduce_scatter x1, waiting for transfers between devices, on_device(): lax.psum_scatter(partial_value, 'shard', scatter_dimension=0, tiled=True)  88.5 us
    all_gather x1, waiting for transfers between devices, on_device(): codes = lax.all_gather(weight_codes, 'shard', axis=0, tiled=True)  54.6 us
    reduce_scatter x1, waiting for transfers between devices, on_device(): lax.psum_scatter(inner, ('node', 'replica'), scatter_dimension=0, tiled=T...  34.2 us
    dot_general x1, matrix products, on_device(): lax.dot_general(tokens, cotangent, (((0,), (0,)), ((), ())), preferred_el...  5.45 us
  transfers between devices with their start and end apart: 3, of which 3 were waited for; matrix products, arithmetic and copies ran while one was open for 2% of the time, Pallas kernels for 0%

commit v1 on v0

--- a/solution.py
+++ b/solution.py
@@ -1,12 +1,20 @@
+import functools
+
 import jax
 import jax.numpy as jnp
 from jax import lax
+from jax.experimental import pallas as pl
+from jax.experimental.pallas import tpu as pltpu
 from jax.sharding import PartitionSpec as P
 
 BLOCK = 128
-
-
-def on_device(tokens, weight_codes, scale_powers, cotangent):
+MESH = pl.DeviceIdType.MESH
+OFF = (2, 1, 3, 0)
+D_, X_, Y_, O_ = 0, 1, 2, 3
+F32, BF16 = jnp.float32, jnp.bfloat16
+
+
+def generic(tokens, weight_codes, scale_powers, cotangent):
     factors = jnp.repeat(jnp.exp2(-scale_powers.astype(jnp.float32)), BLOCK, axis=0)
     codes = lax.all_gather(weight_codes, "shard", axis=0, tiled=True)
     weight = (codes.astype(jnp.float32) * factors).astype(jnp.bfloat16)
@@ -20,6 +28,221 @@
     return (keys_values, weight_grad)
 
 
+def kernel(tokens, codes, scales, cot, kv_out, wg_out,
+           tokv, tokk, cot2, cott, wown, wbuf, s1x, s1y, r1x, r1y,
+           s2x, s2y, r2x, r2y, gown, gx, gy, zs, zr, acc, ls, ss, rs):
+    s, n, r = lax.axis_index("shard"), lax.axis_index("node"), lax.axis_index("replica")
+    xs = s + 1 - 2 * lax.rem(s, 2)
+    ys = s + 2 - 4 * lax.div(s, 2)
+    dest = (3 - s, xs, ys, s)
+    nodes = [lax.rem(n + off, 4) for off in OFF]
+    sib, to_x, to_y = {"replica": 1 - r}, {"shard": xs}, {"shard": ys}
+    to_z = [{"node": nodes[j]} for j in range(3)]
+    T = cot.shape[0]
+
+    nl = [0]
+    sent = []
+
+    def local(src, dst):
+        c = pltpu.make_async_copy(src, dst, ls.at[nl[0]])
+        nl[0] += 1
+        c.start()
+        return c
+
+    def remote(src, dst, device):
+        i = len(sent)
+        c = pltpu.make_async_remote_copy(
+            src_ref=src, dst_ref=dst, send_sem=ss.at[i], recv_sem=rs.at[i],
+            device_id=device, device_id_type=MESH)
+        sent.append(c)
+        c.start()
+        return c
+
+    def columns(d, k, which):
+        return pl.ds(pl.multiple_of(((dest[d] * 4 + nodes[k]) * 2 + which) * 256, 256), 256)
+
+    barrier = pltpu.get_barrier_semaphore()
+    for peer in [sib, to_x, to_y] + to_z:
+        pl.semaphore_signal(barrier, inc=1, device_id=peer, device_id_type=MESH)
+
+    own_tok = {}
+    for k in range(4):
+        for d in (D_, X_, Y_, O_):
+            own_tok[d, k] = local(tokens.at[:, columns(d, k, r)], tokk.at[k * 4 + d, pl.ds(0, T)])
+    load_w = local(codes, wown)
+    load_tok = [None] * 4
+    for d in (O_, X_, Y_, D_):
+        load_tok[d] = local(
+            tokens.at[:, pl.ds(pl.multiple_of(dest[d] * 2048, 2048), 2048)], tokv.at[d])
+    cot2[pl.ds(0, T)] = cot[...]
+
+    pl.semaphore_wait(barrier, 6)
+
+    cot_c = remote(cot, cot2.at[pl.ds(T, T)], sib)
+    sib_tok = {}
+
+    def send_tok(d, k):
+        sib_tok[d, k] = remote(
+            tokens.at[:, columns(d, k, 1 - r)], tokk.at[k * 4 + d, pl.ds(T, T)], sib)
+
+    for d in (D_, X_, Y_):
+        send_tok(d, 0)
+
+    def quarter(q):
+        return pl.ds(pl.multiple_of((2 * r + q) * 512, 512), 512)
+
+    ag = {}
+    ag[X_, 0] = remote(codes.at[quarter(0)], wbuf.at[0, 2 * r + 0], to_x)
+    ag[Y_, 1] = remote(codes.at[quarter(1)], wbuf.at[1, 2 * r + 1], to_y)
+    for k in range(1, 4):
+        for d in (D_, X_, Y_):
+            send_tok(d, k)
+    for k in range(4):
+        send_tok(O_, k)
+    ag[X_, 1] = remote(codes.at[quarter(1)], wbuf.at[0, 2 * r + 1], to_x)
+    ag[Y_, 0] = remote(codes.at[quarter(0)], wbuf.at[1, 2 * r + 0], to_y)
+
+    cot_c.wait_recv()
+    cott[...] = cot2[...].astype(F32).T.astype(BF16)
+
+    def grad(d, k):
+        own_tok[d, k].wait()
+        sib_tok[d, k].wait_recv()
+        return jnp.dot(cott[...], tokk[k * 4 + d], preferred_element_type=F32)
+
+    step1x, step1y, step2x, step2y, zc = {}, {}, {}, {}, {}
+    for k in range(4):
+        g = grad(D_, k)
+        s1x[k, 1] = g[:128].astype(BF16)
+        s1y[k, 1] = g[128:].astype(BF16)
+        g = grad(X_, k)
+        s1x[k, 0] = g[:128].astype(BF16)
+        gx[k] = g[128:]
+        step1x[k] = remote(s1x.at[k], r1x.at[k], to_x)
+        g = grad(Y_, k)
+        s1y[k, 0] = g[128:].astype(BF16)
+        gy[k] = g[:128]
+        step1y[k] = remote(s1y.at[k], r1y.at[k], to_y)
+
+    sw = {}
+
+    def to_sib(d, q):
+        slot = {X_: 0, Y_: 1, D_: 2}[d]
+        sw[d, q] = remote(wbuf.at[slot, 2 * r + q], wbuf.at[slot, 2 * r + q], sib)
+
+    ag[X_, 0].wait_recv()
+    ag[D_, 0] = remote(wbuf.at[0, 2 * r + 0], wbuf.at[2, 2 * r + 0], to_y)
+    to_sib(X_, 0)
+    ag[Y_, 1].wait_recv()
+    ag[D_, 1] = remote(wbuf.at[1, 2 * r + 1], wbuf.at[2, 2 * r + 1], to_x)
+    to_sib(Y_, 1)
+
+    for k in range(4):
+        gown[k] = grad(O_, k)
+
+    def project(d, load):
+        load_tok[d].wait()
+        p = scales[pl.ds(pl.multiple_of(dest[d] * 16, 16), 16), :]
+        fac = jnp.where(p == 5, 2.0 ** -5, jnp.where(p == 6, 2.0 ** -6, jnp.where(p == 7, 2.0 ** -7, 2.0 ** -8))).astype(F32)
+        total = None
+        for c in range(4):
+            w = load(c).astype(F32)
+            w = jnp.concatenate(
+                [w[b * 128:(b + 1) * 128] * fac[c * 4 + b:c * 4 + b + 1, :] for b in range(4)], axis=0
+            ).astype(BF16)
+            part = jnp.dot(tokv[d, :, c * 512:(c + 1) * 512], w, preferred_element_type=F32)
+            total = part if total is None else total + part
+        return total
+
+    load_w.wait()
+    acc[...] = project(O_, lambda c: wown[c * 512:(c + 1) * 512])
+
+    def second(k):
+        step1x[k].wait_recv()
+        s2y[k] = (gy[k] + r1x[k, 1].astype(F32)).astype(BF16)
+        step2y[k] = remote(s2y.at[k], r2y.at[k], to_y)
+        step1y[k].wait_recv()
+        s2x[k] = (gx[k] + r1y[k, 1].astype(F32)).astype(BF16)
+        step2x[k] = remote(s2x.at[k], r2x.at[k], to_x)
+
+    def plane(k):
+        step2y[k].wait_recv()
+        top = gown[k, :128] + r1x[k, 0].astype(F32) + r2y[k].astype(F32)
+        step2x[k].wait_recv()
+        bottom = gown[k, 128:] + r1y[k, 0].astype(F32) + r2x[k].astype(F32)
+        if k < 3:
+            zs[k, :128] = top.astype(BF16)
+            zs[k, 128:] = bottom.astype(BF16)
+            zc[k] = remote(zs.at[k], zr.at[k], to_z[k])
+        else:
+            gown[k, :128] = top
+            gown[k, 128:] = bottom
+
+    def pass_on(d, q):
+        ag[d, q].wait_recv()
+        to_sib(d, q)
+
+    def arrive(d):
+        sw[d, 0].wait_recv()
+        sw[d, 1].wait_recv()
+
+    second(0)
+    pass_on(X_, 1)
+    pass_on(Y_, 0)
+    second(1)
+    plane(0)
+    arrive(X_)
+    acc[...] += project(X_, lambda c: wbuf[0, c])
+    second(2)
+    plane(1)
+    arrive(Y_)
+    acc[...] += project(Y_, lambda c: wbuf[1, c])
+    second(3)
+    plane(2)
+    pass_on(D_, 0)
+    pass_on(D_, 1)
+    plane(3)
+    arrive(D_)
+    kv_out[...] = (acc[...] + project(D_, lambda c: wbuf[2, c])).astype(BF16)
+    total = gown[3]
+    for k in range(3):
+        zc[k].wait_recv()
+        total = total + zr[k].astype(F32)
+    wg_out[...] = total.T
+    for c in sent:
+        c.wait_send()
+
+
+def special(tokens, weight_codes, scale_powers, cotangent):
+    T = tokens.shape[0]
+    vm = pltpu.VMEM
+    n_local, n_remote = 16 + 1 + 4, 49
+    return tuple(pl.pallas_call(
+        kernel,
+        out_shape=(jax.ShapeDtypeStruct((T, 256), BF16), jax.ShapeDtypeStruct((256, 256), F32)),
+        in_specs=[
+            pl.BlockSpec(memory_space=pl.ANY), pl.BlockSpec(memory_space=pl.ANY),
+            pl.BlockSpec(memory_space=vm), pl.BlockSpec(memory_space=vm)],
+        out_specs=(pl.BlockSpec(memory_space=vm), pl.BlockSpec(memory_space=vm)),
+        scratch_shapes=[
+            vm((4, T, 2048), BF16), vm((16, 2 * T, 256), BF16), vm((2 * T, 256), BF16), vm((256, 2 * T), BF16),
+            vm((2048, 256), BF16), vm((3, 4, 512, 256), BF16),
+            vm((4, 2, 128, 256), BF16), vm((4, 2, 128, 256), BF16),
+            vm((4, 2, 128, 256), BF16), vm((4, 2, 128, 256), BF16),
+            vm((4, 128, 256), BF16), vm((4, 128, 256), BF16),
+            vm((4, 128, 256), BF16), vm((4, 128, 256), BF16),
+            vm((4, 256, 256), F32), vm((4, 128, 256), F32), vm((4, 128, 256), F32),
+            vm((3, 256, 256), BF16), vm((3, 256, 256), BF16), vm((T, 256), F32),
+            pltpu.SemaphoreType.DMA((n_local,)),
+            pltpu.SemaphoreType.DMA((n_remote,)),
+            pltpu.SemaphoreType.DMA((n_remote,)),
+        ],
+        compiler_params=pltpu.CompilerParams(
+            collective_id=0, has_side_effects=True, vmem_limit_bytes=40 * 1024 * 1024),
+        cost_estimate=pl.CostEstimate(flops=1_700_000_000, bytes_accessed=6_000_000, transcendentals=0),
+    )(tokens, weight_codes, scale_powers, cotangent))
+
+
 def solution(mesh):
     placed = (
         P(("shard", "node", "replica"), None),
@@ -27,8 +250,9 @@
         P(),
         P(("shard", "node", "replica"), None),
     )
+    small = tuple(mesh.shape[a] for a in ("shard", "node", "replica")) == (4, 4, 2)
     return jax.shard_map(
-        on_device,
+        special if small else generic,
         mesh=mesh,
         in_specs=placed,
         out_specs=(P(("shard", "node", "replica"), None), P(("shard", "node", "replica"), None)),

time: 204 us -> 55.4 us (0.27)
  waiting for transfers between devices: 178 us -> 0 us
  Pallas kernels: 0 us -> 48.2 us
  between operations: 13.8 us -> 0.65 us
  matrix products: 7.16 us -> 0 us
  local copies, waits for them, and re-layouts: 1.85 us -> 6.18 us
  other arithmetic: 3.04 us -> 0 us
    reduce_scatter x2 -> x0, waiting for transfers between devices: 123 us -> none  [the longest x1 88.5 us: on_device(): lax.psum_scatter(partial_value, 'shard', scatter_dimension=0, tiled=True)]
    all_gather x1 -> x0, waiting for transfers between devices: 54.6 us -> none  [on_device(): codes = lax.all_gather(weight_codes, 'shard', axis=0, tiled=True)]
    pallas_call x0 -> x1, Pallas kernels: none -> 48.2 us  [special(): pl.pallas_call(kernel, out_shape=(jax.ShapeDtypeStruct((T, 256), BF16), j...]
    dot_general x2 -> x0, matrix products: 7.16 us -> none  [the longest x1 5.45 us: on_device(): lax.dot_general(tokens, cotangent, (((0,), (0,)), ((), ())), preferred_el...]
    unnamed x4 -> x10, local copies, waits for them, and re-layouts: 1.85 us -> 6.18 us
    convert_element_type x1 -> x0, other arithmetic: 3.02 us -> none  [on_device(): weight = (codes.astype(jnp.float32) * factors).astype(jnp.bfloat16)]
  transfers between devices with their start and end apart: 3 -> 0, of which waited for: 3 -> 0; matrix products, arithmetic and copies ran while one was open for 2% -> 0% of each run, Pallas kernels for 0% -> 0%
where the time goes in v1:
time: 55.4 us; the launch traced here: 55.1 us
  Pallas kernels  48.2 us (87%)
  local copies, waits for them, and re-layouts  6.18 us (11%)
  between operations  0.65 us (1%)
    pallas_call x1, Pallas kernels, special(): pl.pallas_call(kernel, out_shape=(jax.ShapeDtypeStruct((T, 256), BF16), j...  48.2 us
    unnamed x10, local copies, waits for them, and re-layouts  6.18 us

profile of v1, /device:TPU:0, one launch (start us, length us, event | category | flops | bytes accessed | tf_op | source)
XLA Modules:
  0.0 55.1 jit_solution(7478904835974512441)
XLA Ops:
  0.6 0.0 copy-start
  0.6 1.9 %copy-done = bf16[192,8192]{1,0:T(8,128)(2,1)S(1)} copy-done((bf16[192,8192]{1,0:T(8,128)(2,1)S(1)}, bf16[192,8192]{1,0:T(8,128)(2,1)}, u32[]{:S(2)}) %copy-start) | copy-done | bytes 3145752
  2.5 0.0 copy-start.1
  2.5 1.2 %copy-done.1 = bf16[2048,256]{1,0:T(8,128)(2,1)S(1)} copy-done((bf16[2048,256]{1,0:T(8,128)(2,1)S(1)}, bf16[2048,256]{1,0:T(8,128)(2,1)}, u32[]{:S(2)}) %copy-start.1) | copy-done | bytes 1048600
  3.7 0.0 copy-start.2
  3.7 0.9 %copy-done.2 = bf16[192,256]{1,0:T(8,128)(2,1)S(1)} copy-done((bf16[192,256]{1,0:T(8,128)(2,1)S(1)}, bf16[192,256]{1,0:T(8,128)(2,1)}, u32[]{:S(2)}) %copy-start.2) | copy-done | bytes 98328
  4.6 0.0 copy-start.3
  4.6 0.8 %copy-done.3 = s32[64,256]{1,0:T(8,128)S(1)} copy-done((s32[64,256]{1,0:T(8,128)S(1)}, s32[64,256]{1,0:T(8,128)}, u32[]{:S(2)}) %copy-start.3) | copy-done | bytes 65560
  5.5 48.2 %shard_map.59 = (bf16[192,256]{1,0:T(8,128)(2,1)S(1)}, f32[256,256]{1,0:T(8,128)S(1)}) custom-call(bf16[192,8192]{1,0:T(8,128)(2,1)S(1)} %copy-done, bf16[2048,256]{1,0:T(8,128)(2,1)S(1)} %copy-done.1, s32[64,256]{1,0:T(8,128)S(1)} %copy-done.3, bf16[192,256]{1,0:T(8,128)(2,1)S(1)} %copy-done.2), custom_call_target="tpu_custom_call" | custom-call | flops 1700000000 | bytes 6000000 | tf_op jit(solution)/shard_map/pallas_call | solution.py:220
  53.7 0.6 %copy.8 = bf16[192,256]{1,0:T(8,128)(2,1)} copy(bf16[192,256]{1,0:T(8,128)(2,1)S(1)} %get-tuple-element.4) | data formatting | bytes 196608
  54.4 0.7 %copy.9 = f32[256,256]{1,0:T(8,128)} copy(f32[256,256]{1,0:T(8,128)S(1)} %get-tuple-element.5) | data formatting | bytes 524288
Async XLA Ops:
  0.6 1.9 %copy-start = (bf16[192,8192]{1,0:T(8,128)(2,1)S(1)}, bf16[192,8192]{1,0:T(8,128)(2,1)}, u32[]{:S(2)}) copy-start(bf16[192,8192]{1,0:T(8,128)(2,1)} %tokens.1) | copy-start | bytes 9437188
  2.5 1.2 %copy-start.1 = (bf16[2048,256]{1,0:T(8,128)(2,1)S(1)}, bf16[2048,256]{1,0:T(8,128)(2,1)}, u32[]{:S(2)}) copy-start(bf16[2048,256]{1,0:T(8,128)(2,1)} %codes.1) | copy-start | bytes 3145732
  3.7 0.9 %copy-start.2 = (bf16[192,256]{1,0:T(8,128)(2,1)S(1)}, bf16[192,256]{1,0:T(8,128)(2,1)}, u32[]{:S(2)}) copy-start(bf16[192,256]{1,0:T(8,128)(2,1)} %cot.1) | copy-start | bytes 294916
  4.6 0.8 %copy-start.3 = (s32[64,256]{1,0:T(8,128)S(1)}, s32[64,256]{1,0:T(8,128)}, u32[]{:S(2)}) copy-start(s32[64,256]{1,0:T(8,128)} %scales.1) | copy-start | bytes 196612

commit v2 on v1

--- a/solution.py
+++ b/solution.py
@@ -28,9 +28,9 @@
     return (keys_values, weight_grad)
 
 
-def kernel(tokens, codes, scales, cot, kv_out, wg_out,
+def kernel(tokens, codes, scales_in, cot, kv_out, wg_out,
            tokv, tokk, cot2, cott, wown, wbuf, s1x, s1y, r1x, r1y,
-           s2x, s2y, r2x, r2y, gown, gx, gy, zs, zr, acc, ls, ss, rs):
+           s2x, s2y, r2x, r2y, gown, gx, gy, zs, zr, acc, scales, ls, ss, rs):
     s, n, r = lax.axis_index("shard"), lax.axis_index("node"), lax.axis_index("replica")
     xs = s + 1 - 2 * lax.rem(s, 2)
     ys = s + 2 - 4 * lax.div(s, 2)
@@ -39,6 +39,9 @@
     sib, to_x, to_y = {"replica": 1 - r}, {"shard": xs}, {"shard": ys}
     to_z = [{"node": nodes[j]} for j in range(3)]
     T = cot.shape[0]
+    par = lax.rem(n, 2)
+    mine, theirs = 2 * r + par, 2 * r + 1 - par
+    to_pair = {"node": n + 1 - 2 * par}
 
     nl = [0]
     sent = []
@@ -65,6 +68,8 @@
     for peer in [sib, to_x, to_y] + to_z:
         pl.semaphore_signal(barrier, inc=1, device_id=peer, device_id_type=MESH)
 
+    load_cot = local(cot, cot2.at[pl.ds(0, T)])
+    load_sc = local(scales_in, scales)
     own_tok = {}
     for k in range(4):
         for d in (D_, X_, Y_, O_):
@@ -74,7 +79,6 @@
     for d in (O_, X_, Y_, D_):
         load_tok[d] = local(
             tokens.at[:, pl.ds(pl.multiple_of(dest[d] * 2048, 2048), 2048)], tokv.at[d])
-    cot2[pl.ds(0, T)] = cot[...]
 
     pl.semaphore_wait(barrier, 6)
 
@@ -88,20 +92,17 @@
     for d in (D_, X_, Y_):
         send_tok(d, 0)
 
-    def quarter(q):
-        return pl.ds(pl.multiple_of((2 * r + q) * 512, 512), 512)
-
+    rows = pl.ds(pl.multiple_of(mine * 512, 512), 512)
     ag = {}
-    ag[X_, 0] = remote(codes.at[quarter(0)], wbuf.at[0, 2 * r + 0], to_x)
-    ag[Y_, 1] = remote(codes.at[quarter(1)], wbuf.at[1, 2 * r + 1], to_y)
+    ag[X_] = remote(codes.at[rows], wbuf.at[0, mine], to_x)
+    ag[Y_] = remote(codes.at[rows], wbuf.at[1, mine], to_y)
     for k in range(1, 4):
         for d in (D_, X_, Y_):
             send_tok(d, k)
     for k in range(4):
         send_tok(O_, k)
-    ag[X_, 1] = remote(codes.at[quarter(1)], wbuf.at[0, 2 * r + 1], to_x)
-    ag[Y_, 0] = remote(codes.at[quarter(0)], wbuf.at[1, 2 * r + 0], to_y)
-
+
+    load_cot.wait()
     cot_c.wait_recv()
     cott[...] = cot2[...].astype(F32).T.astype(BF16)
 
@@ -111,6 +112,17 @@
         return jnp.dot(cott[...], tokk[k * 4 + d], preferred_element_type=F32)
 
     step1x, step1y, step2x, step2y, zc = {}, {}, {}, {}, {}
+    slot = {X_: 0, Y_: 1, D_: 2}
+    pair, sw = {}, {}
+
+    def spread(d):
+        pair[d] = remote(wbuf.at[slot[d], mine], wbuf.at[slot[d], mine], to_pair)
+        sw[d, 0] = remote(wbuf.at[slot[d], mine], wbuf.at[slot[d], mine], sib)
+
+    def pass_on(d):
+        pair[d].wait_recv()
+        sw[d, 1] = remote(wbuf.at[slot[d], theirs], wbuf.at[slot[d], theirs], sib)
+
     for k in range(4):
         g = grad(D_, k)
         s1x[k, 1] = g[:128].astype(BF16)
@@ -123,22 +135,14 @@
         s1y[k, 0] = g[128:].astype(BF16)
         gy[k] = g[:128]
         step1y[k] = remote(s1y.at[k], r1y.at[k], to_y)
-
-    sw = {}
-
-    def to_sib(d, q):
-        slot = {X_: 0, Y_: 1, D_: 2}[d]
-        sw[d, q] = remote(wbuf.at[slot, 2 * r + q], wbuf.at[slot, 2 * r + q], sib)
-
-    ag[X_, 0].wait_recv()
-    ag[D_, 0] = remote(wbuf.at[0, 2 * r + 0], wbuf.at[2, 2 * r + 0], to_y)
-    to_sib(X_, 0)
-    ag[Y_, 1].wait_recv()
-    ag[D_, 1] = remote(wbuf.at[1, 2 * r + 1], wbuf.at[2, 2 * r + 1], to_x)
-    to_sib(Y_, 1)
-
-    for k in range(4):
-        gown[k] = grad(O_, k)
+        if k == 1:
+            top, bottom = pl.ds(0, 256), pl.ds(256, 256)
+            ag[X_].wait_recv()
+            ag[D_, 0] = remote(wbuf.at[0, mine, top], wbuf.at[2, mine, top], to_y)
+            ag[Y_].wait_recv()
+            ag[D_, 1] = remote(wbuf.at[1, mine, bottom], wbuf.at[2, mine, bottom], to_x)
+            spread(X_)
+            spread(Y_)
 
     def project(d, load):
         load_tok[d].wait()
@@ -154,9 +158,6 @@
             total = part if total is None else total + part
         return total
 
-    load_w.wait()
-    acc[...] = project(O_, lambda c: wown[c * 512:(c + 1) * 512])
-
     def second(k):
         step1x[k].wait_recv()
         s2y[k] = (gy[k] + r1x[k, 1].astype(F32)).astype(BF16)
@@ -178,32 +179,35 @@
             gown[k, :128] = top
             gown[k, 128:] = bottom
 
-    def pass_on(d, q):
-        ag[d, q].wait_recv()
-        to_sib(d, q)
-
     def arrive(d):
         sw[d, 0].wait_recv()
         sw[d, 1].wait_recv()
 
+    for k in range(4):
+        gown[k] = grad(O_, k)
     second(0)
-    pass_on(X_, 1)
-    pass_on(Y_, 0)
+    ag[D_, 0].wait_recv()
+    ag[D_, 1].wait_recv()
+    spread(D_)
     second(1)
+    pass_on(X_)
+    pass_on(Y_)
     plane(0)
+    load_w.wait()
+    load_sc.wait()
+    acc[...] = project(O_, lambda c: wown[c * 512:(c + 1) * 512])
+    second(2)
+    plane(1)
     arrive(X_)
     acc[...] += project(X_, lambda c: wbuf[0, c])
-    second(2)
-    plane(1)
+    second(3)
+    pass_on(D_)
+    plane(2)
     arrive(Y_)
     acc[...] += project(Y_, lambda c: wbuf[1, c])
-    second(3)
-    plane(2)
-    pass_on(D_, 0)
-    pass_on(D_, 1)
-    plane(3)
     arrive(D_)
     kv_out[...] = (acc[...] + project(D_, lambda c: wbuf[2, c])).astype(BF16)
+    plane(3)
     total = gown[3]
     for k in range(3):
         zc[k].wait_recv()
@@ -216,13 +220,13 @@
 def special(tokens, weight_codes, scale_powers, cotangent):
     T = tokens.shape[0]
     vm = pltpu.VMEM
-    n_local, n_remote = 16 + 1 + 4, 49
+    n_local, n_remote = 16 + 1 + 4 + 2, 49
     return tuple(pl.pallas_call(
         kernel,
         out_shape=(jax.ShapeDtypeStruct((T, 256), BF16), jax.ShapeDtypeStruct((256, 256), F32)),
         in_specs=[
             pl.BlockSpec(memory_space=pl.ANY), pl.BlockSpec(memory_space=pl.ANY),
-            pl.BlockSpec(memory_space=vm), pl.BlockSpec(memory_space=vm)],
+            pl.BlockSpec(memory_space=pl.ANY), pl.BlockSpec(memory_space=pl.ANY)],
         out_specs=(pl.BlockSpec(memory_space=vm), pl.BlockSpec(memory_space=vm)),
         scratch_shapes=[
             vm((4, T, 2048), BF16), vm((16, 2 * T, 256), BF16), vm((2 * T, 256), BF16), vm((256, 2 * T), BF16),
@@ -233,12 +237,13 @@
             vm((4, 128, 256), BF16), vm((4, 128, 256), BF16),
             vm((4, 256, 256), F32), vm((4, 128, 256), F32), vm((4, 128, 256), F32),
             vm((3, 256, 256), BF16), vm((3, 256, 256), BF16), vm((T, 256), F32),
+            vm((64, 256), jnp.int32),
             pltpu.SemaphoreType.DMA((n_local,)),
             pltpu.SemaphoreType.DMA((n_remote,)),
             pltpu.SemaphoreType.DMA((n_remote,)),
         ],
         compiler_params=pltpu.CompilerParams(
-            collective_id=0, has_side_effects=True, vmem_limit_bytes=40 * 1024 * 1024),
+            collective_id=0, has_side_effects=True, vmem_limit_bytes=64 * 1024 * 1024 - 65536),
         cost_estimate=pl.CostEstimate(flops=1_700_000_000, bytes_accessed=6_000_000, transcendentals=0),
     )(tokens, weight_codes, scale_powers, cotangent))
 

time: 55.4 us -> 45 us (0.81)
  Pallas kernels: 48.2 us -> 40.9 us
  local copies, waits for them, and re-layouts: 6.18 us -> 3.21 us
    pallas_call x1, Pallas kernels: 48.2 us -> 40.9 us  [special(): pl.pallas_call(kernel, out_shape=(jax.ShapeDtypeStruct((T, 256), BF16), j...]
    unnamed x10 -> x2, local copies, waits for them, and re-layouts: 6.18 us -> 3.21 us
where the time goes in v2:
time: 45 us; the launch traced here: 44.8 us
  Pallas kernels  40.9 us (91%)
  local copies, waits for them, and re-layouts  3.21 us (7%)
  between operations  0.64 us (1%)
    pallas_call x1, Pallas kernels, special(): pl.pallas_call(kernel, out_shape=(jax.ShapeDtypeStruct((T, 256), BF16), j...  40.9 us
    unnamed x2, local copies, waits for them, and re-layouts  3.21 us

profile of v2, /device:TPU:0, one launch (start us, length us, event | category | flops | bytes accessed | tf_op | source)
XLA Modules:
  0.0 44.8 jit_solution(1577420608710529716)
XLA Ops:
  0.6 40.9 %shard_map.59 = (bf16[192,256]{1,0:T(8,128)(2,1)}, f32[256,256]{1,0:T(8,128)}) custom-call(bf16[192,8192]{1,0:T(8,128)(2,1)} %tokens.1, bf16[2048,256]{1,0:T(8,128)(2,1)} %codes.1, s32[64,256]{1,0:T(8,128)} %scales_in.1, bf16[192,256]{1,0:T(8,128)(2,1)} %cot.1), custom_call_target="tpu_custom_call" | custom-call | flops 1700000000 | bytes 6000000 | tf_op jit(solution)/shard_map/pallas_call | solution.py:224
  41.6 1.5 %copy.8 = bf16[192,256]{1,0:T(8,128)(2,1)} copy(bf16[192,256]{1,0:T(8,128)(2,1)} %get-tuple-element.4) | data formatting | bytes 196608
  43.1 1.7 %copy.9 = f32[256,256]{1,0:T(8,128)} copy(f32[256,256]{1,0:T(8,128)} %get-tuple-element.5) | data formatting | bytes 524288

commit v3 on v2

--- a/solution.py
+++ b/solution.py
@@ -72,36 +72,39 @@
     load_sc = local(scales_in, scales)
     own_tok = {}
     for k in range(4):
-        for d in (D_, X_, Y_, O_):
+        for d in (D_, X_, Y_):
             own_tok[d, k] = local(tokens.at[:, columns(d, k, r)], tokk.at[k * 4 + d, pl.ds(0, T)])
+    pl.semaphore_wait(barrier, 6)
+
+    cot_c = remote(cot, cot2.at[pl.ds(T, T)], sib)
+    sib_tok = {}
+
+    def send_tok(d, k):
+        sib_tok[d, k] = remote(
+            tokens.at[:, columns(d, k, 1 - r)], tokk.at[k * 4 + d, pl.ds(T, T)], sib)
+
+    for d in (D_, X_, Y_):
+        send_tok(d, 0)
+
+    half = (pl.ds(0, 256), pl.ds(256, 256))
+    ag = {}
+    for d, h in ((X_, 0), (Y_, 1), (X_, 1), (Y_, 0)):
+        rows = pl.ds(pl.multiple_of(mine * 512 + h * 256, 256), 256)
+        ag[d, h] = remote(codes.at[rows], wbuf.at[d - 1, mine, half[h]], to_x if d == X_ else to_y)
+    for k in range(1, 4):
+        for d in (D_, X_, Y_):
+            send_tok(d, k)
+    for k in range(4):
+        send_tok(O_, k)
+
+    for k in range(4):
+        own_tok[O_, k] = local(tokens.at[:, columns(O_, k, r)], tokk.at[k * 4 + O_, pl.ds(0, T)])
     load_w = local(codes, wown)
     load_tok = [None] * 4
     for d in (O_, X_, Y_, D_):
         load_tok[d] = local(
             tokens.at[:, pl.ds(pl.multiple_of(dest[d] * 2048, 2048), 2048)], tokv.at[d])
 
-    pl.semaphore_wait(barrier, 6)
-
-    cot_c = remote(cot, cot2.at[pl.ds(T, T)], sib)
-    sib_tok = {}
-
-    def send_tok(d, k):
-        sib_tok[d, k] = remote(
-            tokens.at[:, columns(d, k, 1 - r)], tokk.at[k * 4 + d, pl.ds(T, T)], sib)
-
-    for d in (D_, X_, Y_):
-        send_tok(d, 0)
-
-    rows = pl.ds(pl.multiple_of(mine * 512, 512), 512)
-    ag = {}
-    ag[X_] = remote(codes.at[rows], wbuf.at[0, mine], to_x)
-    ag[Y_] = remote(codes.at[rows], wbuf.at[1, mine], to_y)
-    for k in range(1, 4):
-        for d in (D_, X_, Y_):
-            send_tok(d, k)
-    for k in range(4):
-        send_tok(O_, k)
-
     load_cot.wait()
     cot_c.wait_recv()
     cott[...] = cot2[...].astype(F32).T.astype(BF16)
@@ -115,13 +118,31 @@
     slot = {X_: 0, Y_: 1, D_: 2}
     pair, sw = {}, {}
 
-    def spread(d):
-        pair[d] = remote(wbuf.at[slot[d], mine], wbuf.at[slot[d], mine], to_pair)
-        sw[d, 0] = remote(wbuf.at[slot[d], mine], wbuf.at[slot[d], mine], sib)
+    def spread(d, h):
+        ag[d, h].wait_recv()
+        piece = wbuf.at[slot[d], mine, half[h]]
+        if (d, h) == (X_, 0):
+            ag[D_, 0] = remote(piece, wbuf.at[2, mine, half[0]], to_y)
+        if (d, h) == (Y_, 1):
+            ag[D_, 1] = remote(piece, wbuf.at[2, mine, half[1]], to_x)
+        pair[d, h] = remote(piece, piece, to_pair)
+        sw[d, h, 0] = remote(piece, piece, sib)
 
     def pass_on(d):
-        pair[d].wait_recv()
-        sw[d, 1] = remote(wbuf.at[slot[d], theirs], wbuf.at[slot[d], theirs], sib)
+        for h in (0, 1):
+            pair[d, h].wait_recv()
+            piece = wbuf.at[slot[d], theirs, half[h]]
+            sw[d, h, 1] = remote(piece, piece, sib)
+
+    left = []
+
+    def first(k):
+        if k >= 2:
+            for c in (step1x[k - 2], step1y[k - 2]):
+                c.wait_send()
+                left.append(c)
+        step1x[k] = remote(s1x.at[k], r1x.at[k], to_x)
+        step1y[k] = remote(s1y.at[k], r1y.at[k], to_y)
 
     for k in range(4):
         g = grad(D_, k)
@@ -130,19 +151,17 @@
         g = grad(X_, k)
         s1x[k, 0] = g[:128].astype(BF16)
         gx[k] = g[128:]
-        step1x[k] = remote(s1x.at[k], r1x.at[k], to_x)
         g = grad(Y_, k)
         s1y[k, 0] = g[128:].astype(BF16)
         gy[k] = g[:128]
-        step1y[k] = remote(s1y.at[k], r1y.at[k], to_y)
+        if k < 2:
+            first(k)
+        if k == 0:
+            spread(X_, 0)
+            spread(Y_, 1)
         if k == 1:
-            top, bottom = pl.ds(0, 256), pl.ds(256, 256)
-            ag[X_].wait_recv()
-            ag[D_, 0] = remote(wbuf.at[0, mine, top], wbuf.at[2, mine, top], to_y)
-            ag[Y_].wait_recv()
-            ag[D_, 1] = remote(wbuf.at[1, mine, bottom], wbuf.at[2, mine, bottom], to_x)
-            spread(X_)
-            spread(Y_)
+            spread(X_, 1)
+            spread(Y_, 0)
 
     def project(d, load):
         load_tok[d].wait()
@@ -180,47 +199,50 @@
             gown[k, 128:] = bottom
 
     def arrive(d):
-        sw[d, 0].wait_recv()
-        sw[d, 1].wait_recv()
-
+        for h in (0, 1):
+            sw[d, h, 0].wait_recv()
+            sw[d, h, 1].wait_recv()
+
+    first(2)
     for k in range(4):
         gown[k] = grad(O_, k)
+    spread(D_, 0)
+    spread(D_, 1)
     second(0)
-    ag[D_, 0].wait_recv()
-    ag[D_, 1].wait_recv()
-    spread(D_)
+    first(3)
     second(1)
-    pass_on(X_)
-    pass_on(Y_)
     plane(0)
     load_w.wait()
     load_sc.wait()
     acc[...] = project(O_, lambda c: wown[c * 512:(c + 1) * 512])
     second(2)
     plane(1)
+    pass_on(X_)
+    pass_on(Y_)
+    second(3)
+    plane(2)
+    pass_on(D_)
     arrive(X_)
     acc[...] += project(X_, lambda c: wbuf[0, c])
-    second(3)
-    pass_on(D_)
-    plane(2)
     arrive(Y_)
     acc[...] += project(Y_, lambda c: wbuf[1, c])
+    plane(3)
     arrive(D_)
     kv_out[...] = (acc[...] + project(D_, lambda c: wbuf[2, c])).astype(BF16)
-    plane(3)
     total = gown[3]
     for k in range(3):
         zc[k].wait_recv()
         total = total + zr[k].astype(F32)
     wg_out[...] = total.T
     for c in sent:
-        c.wait_send()
+        if all(c is not done for done in left):
+            c.wait_send()
 
 
 def special(tokens, weight_codes, scale_powers, cotangent):
     T = tokens.shape[0]
     vm = pltpu.VMEM
-    n_local, n_remote = 16 + 1 + 4 + 2, 49
+    n_local, n_remote = 16 + 1 + 4 + 2, 60
     return tuple(pl.pallas_call(
         kernel,
         out_shape=(jax.ShapeDtypeStruct((T, 256), BF16), jax.ShapeDtypeStruct((256, 256), F32)),

time: 45 us -> 44 us (0.978)
  Pallas kernels: 40.9 us -> 39.9 us
    pallas_call x1, Pallas kernels: 40.9 us -> 39.9 us  [special(): pl.pallas_call(kernel, out_shape=(jax.ShapeDtypeStruct((T, 256), BF16), j...]
where the time goes in v3:
time: 44 us; the launch traced here: 43.8 us
  Pallas kernels  39.9 us (91%)
  local copies, waits for them, and re-layouts  3.21 us (7%)
  between operations  0.64 us (1%)
    pallas_call x1, Pallas kernels, special(): pl.pallas_call(kernel, out_shape=(jax.ShapeDtypeStruct((T, 256), BF16), j...  39.9 us
    unnamed x2, local copies, waits for them, and re-layouts  3.21 us

profile of v3, /device:TPU:0, one launch (start us, length us, event | category | flops | bytes accessed | tf_op | source)
XLA Modules:
  0.0 43.8 jit_solution(741975569795059973)
XLA Ops:
  0.6 39.9 %shard_map.59 = (bf16[192,256]{1,0:T(8,128)(2,1)}, f32[256,256]{1,0:T(8,128)}) custom-call(bf16[192,8192]{1,0:T(8,128)(2,1)} %tokens.1, bf16[2048,256]{1,0:T(8,128)(2,1)} %codes.1, s32[64,256]{1,0:T(8,128)} %scales_in.1, bf16[192,256]{1,0:T(8,128)(2,1)} %cot.1), custom_call_target="tpu_custom_call" | custom-call | flops 1700000000 | bytes 6000000 | tf_op jit(solution)/shard_map/pallas_call | solution.py:246
  40.6 1.5 %copy.8 = bf16[192,256]{1,0:T(8,128)(2,1)} copy(bf16[192,256]{1,0:T(8,128)(2,1)} %get-tuple-element.4) | data formatting | bytes 196608
  42.1 1.7 %copy.9 = f32[256,256]{1,0:T(8,128)} copy(f32[256,256]{1,0:T(8,128)} %get-tuple-element.5) | data formatting | bytes 524288
